TPU v7x, 256 devices: a whole 4x4x8 slice. The times are simulated.
256 devices in a mesh: dom: 32 (over z, x), col: 8 (over y, core).
Axes of the slice: x: 4, y: 4, z: 8, core: 2. Of those that a mesh axis runs over, the one named last changes fastest.
Arguments:
- features: bfloat16 [65536, 128], P(('dom', 'col'))
- w_hidden: bfloat16 [128, 256], replicated, may hold values from -0.5 to 0.5
- w_out: bfloat16 [256, 256], replicated, may hold values from -0.375 to 0.375
- block_values: bfloat16 [8192, 4096], P('dom'), may hold values from 0.0009994507 to 1
- block_slot: int32 [8192], P('dom'), may hold values from 0 to 159, as said below
- requested: int32 [32, 32, 4], P('dom'), may hold values from -1 to 31, as said below
- labels: int32 [65536], P('dom'), may hold values from 0 to 171
- train_mask: int32 [65536], P('dom'), may hold values 0 or 1
Outputs:
- propagated: float32 [256, 65536], P('col', 'dom')
- logit_grad: float32 [256, 65536], P('col', 'dom')
Inputs may be any that keep to these rules, and one draw needn't show every extreme that they name: requested[q, p, :] lists distinct row blocks of partition p first and -1 for the rest; it is all -1 for p = q and has at least one entry for every other p; for each q some p has all 4 entries. `block_slot`: each slot s >= 32 that a block of partition q names has requested[q, (s - 32) // 4, (s - 32) % 4] >= 0, and every such entry of requested is named by exactly one block of q; partition 0 reads 4 blocks from the last partition.
All inputs are finite; a program needn't handle non-finite values. No bound on the sum of `train_mask` on one device may be relied on, other than what follows from the above.
Results may differ from a plain program's by a relative error of at most 0.0037.
Values may be sent and summed in bfloat16 or wider, within the bound.
A program may use at most 64 MiB of HBM per device.

v0:
```python
import functools
import math

import jax
import jax.numpy as jnp
from jax import lax
from jax.experimental import pallas as pl
from jax.experimental.pallas import tpu as pltpu
from jax.sharding import PartitionSpec as P

NCLASS = 172
BLOCK = 64
STEPS = 3
CAP = 4
TELEPORT = 0.1
FILL = -1e30

HALF = 16
LANES = 128
HALVES = 2
PAIRS = CAP // 2
SPREAD = 32
GROUP = 8

F32 = jnp.float32
BF16 = jnp.bfloat16
MESH = pl.DeviceIdType.MESH


def index_tables(block_slot, doms, row_blocks):
    entries = block_slot.shape[0]
    me = lax.axis_index("dom")
    chunks = -(-((entries - (doms - 1) + row_blocks) // 2) // GROUP) * GROUP
    near = row_blocks // 2 + 1
    far = row_blocks // 2 + (doms - 1) * PAIRS
    entry = jnp.arange(entries, dtype=jnp.int32)
    blocks = jnp.arange(row_blocks, dtype=jnp.int32)
    local = block_slot < row_blocks
    peer = (block_slot - row_blocks) // CAP
    place = (block_slot - row_blocks) % CAP
    came = jnp.where(local, block_slot, row_blocks + ((me - peer - 1) % doms) * CAP + place)
    came = came // 2 + jnp.where(came % 2 == entry % 2, 0, far)
    goes = jnp.where(local, -1, ((peer - me - 1) % doms) * CAP + place)
    slots = jnp.arange(doms * CAP, dtype=jnp.int32)
    entry_of = jnp.sum(jnp.where(goes[None, :] == slots[:, None], entry[None, :], 0), axis=1)
    row_of = entry_of // 8
    count = jnp.sum((block_slot[None, :] == blocks[:, None]).astype(jnp.int32), axis=1)
    pairs = (count + 1) // 2
    first = jnp.sum(jnp.where(blocks[None, :] < blocks[:, None], pairs[None, :], 0), axis=1)
    before = jnp.sum(jnp.where(blocks[None, :] < block_slot[:, None], pairs[None, :], 0), axis=1)
    same = (block_slot[None, :] == block_slot[:, None]) & (entry[None, :] < entry[:, None])
    rank = jnp.sum(same.astype(jnp.int32), axis=1)
    at = jnp.where(local, 2 * before + rank, -1)
    spots = jnp.arange(2 * chunks, dtype=jnp.int32)
    coded = 2 * entry + block_slot % 2 + 1
    order = jnp.sum(jnp.where(at[None, :] == spots[:, None], coded[None, :], 0), axis=1) - 1
    used = jnp.maximum(order, 0) // 2
    row = used // 8
    chunk = jnp.arange(chunks, dtype=jnp.int32)
    starts = (first[None, :] == chunk[:, None]) & (count[None, :] > 0)
    keep = 1 - jnp.max(starts.astype(jnp.int32), axis=1)
    lists = (
        came,
        entry_of // 2,
        slots % 2 + jnp.where(entry_of % 2 == slots % 2, 0, 4),
        row_of // 2 + jnp.where(row_of % 2 == slots % 2, 0, near),
        used // 2,
        jnp.where(order < 0, 2, order % 2 + jnp.where(used % 2 == order % 2, 0, 4)),
        row // 2 + jnp.where(row % 2 == spots % 2, 0, near),
        keep,
        jnp.where(count > 0, first + pairs - 1, chunks),
    )
    return jnp.concatenate([x.astype(jnp.int32) for x in lists]), chunks


def kernel(
    doms,
    cols,
    classes,
    chunks,
    index,
    features,
    w_hidden,
    w_out,
    values,
    request,
    code,
    prop_out,
    grad_out,
    features_here,
    hidden_here,
    out_here,
    values_here,
    by_entry,
    by_row,
    tiles,
    head_send,
    stat_send,
    stat_recv,
    want,
    want_s,
    teleports,
    table00,
    table01,
    table10,
    table11,
    table20,
    table21,
    near0,
    near1,
    inverse,
    final,
    grad,
    acc,
    come_in,
    remote_tiles,
    local_tiles,
    route,
    out_buf,
    back_buf,
    head_sems,
    stat_sems,
    request_sems,
    local_sems,
    send_sems,
    recv_sems,
):
    me = lax.axis_index("dom")
    my_col = lax.axis_index("col")
    row_pairs = code.shape[0]
    row_blocks = 2 * row_pairs
    entries = row_blocks * 8
    share = w_out.shape[1] // cols
    mine = features.shape[0] // LANES
    peers = doms - 1
    slots, spots = doms * CAP, 2 * chunks
    at_slot_tile = entries
    at_slot_side = at_slot_tile + slots
    at_slot_row = at_slot_side + slots
    at_tile = at_slot_row + slots
    at_side = at_tile + spots
    at_row = at_side + spots
    at_keep = at_row + spots
    at_last = at_keep + chunks
    near_pairs = row_pairs + 1
    far_pairs = row_pairs + peers * PAIRS
    pair_group = GROUP // 2
    table = ((table00, table01), (table10, table11), (table20, table21))
    near = (near0, near1)

    low = lax.broadcasted_iota(jnp.int32, (HALF, LANES), 1) < BLOCK

    def swap(x):
        return pltpu.roll(x, BLOCK, 1)

    def turn(blocks):
        count = blocks.shape[0]
        flat = swap(blocks.astype(F32).reshape(count * HALF, LANES))
        return flat.astype(BF16).reshape(count, HALF, LANES)

    def dom_at(shift):
        return lax.rem(me + shift, doms)

    def col_at(shift):
        return lax.rem(my_col + shift, cols)

    stride = 12 if math.gcd(12, peers) == 1 else 1

    def mixed(i):
        return lax.rem(i * stride + peers // 2, peers)

    loads = [
        pltpu.make_async_copy(src, dst, local_sems.at[i])
        for i, (src, dst) in enumerate(
            ((features, features_here), (w_hidden, hidden_here), (w_out, out_here), (values, values_here))
        )
    ]
    for load in loads:
        load.start()

    barrier = pltpu.get_barrier_semaphore()

    def greet_dom(k, carry):
        pl.semaphore_signal(barrier, inc=1, device_id={"dom": dom_at(k + 1)}, device_id_type=MESH)
        return carry

    def greet_col(k, carry):
        pl.semaphore_signal(barrier, inc=1, device_id={"col": col_at(k + 1)}, device_id_type=MESH)
        return carry

    lax.fori_loop(0, peers, greet_dom, 0)
    lax.fori_loop(0, cols - 1, greet_col, 0)

    for load in loads[:3]:
        load.wait()
    hidden = jax.nn.relu(jnp.dot(features_here[...], hidden_here[...], preferred_element_type=F32)).astype(BF16)
    heads = jnp.dot(hidden, out_here[...], preferred_element_type=F32).T.astype(BF16)
    for c in range(cols):
        for pair in range(mine):
            for u in range(HALVES):
                first = c * share + u * HALF
                head_send[c * mine + pair, u] = heads[first : first + HALF, pair * LANES : (pair + 1) * LANES]

    pl.semaphore_wait(barrier, peers + cols - 1)

    def request_copy(k):
        return pltpu.make_async_remote_copy(
            src_ref=request.at[dom_at(k + 1)],
            dst_ref=want.at[k],
            send_sem=request_sems.at[0],
            recv_sem=request_sems.at[1],
            device_id={"dom": dom_at(k + 1)},
            device_id_type=MESH,
        )

    def start_request(k, carry):
        request_copy(k).start()
        return carry

    lax.fori_loop(0, peers, start_request, 0)

    def own(col):
        return pl.ds(col * mine, mine)

    def head_copy(j):
        return pltpu.make_async_remote_copy(
            src_ref=head_send.at[own(col_at(j + 1))],
            dst_ref=teleports.at[own(my_col)],
            send_sem=head_sems.at[0, j],
            recv_sem=head_sems.at[1, j],
            device_id={"col": col_at(j + 1)},
            device_id_type=MESH,
        )

    for j in range(cols - 1):
        head_copy(j).start()
    teleports[own(my_col)] = head_send[own(my_col)]

    def all_requests():
        return pltpu.make_async_remote_copy(
            src_ref=want.at[pl.ds(0, peers)],
            dst_ref=want.at[pl.ds(0, peers)],
            send_sem=request_sems.at[0],
            recv_sem=request_sems.at[1],
            device_id={"dom": dom_at(1)},
            device_id_type=MESH,
        )

    all_requests().wait_recv()
    want[peers] = jnp.full((1, LANES), row_pairs, jnp.int32)
    to_scalars = pltpu.make_async_copy(want, want_s, local_sems.at[4])
    to_scalars.start()
    for u in range(HALVES):
        near[u][row_pairs] = jnp.zeros((HALF, LANES), BF16)
    for j in range(cols - 1):
        head_copy(j).wait_recv()

    def keep_state(step, u, at, later, blocks):
        flipped = turn(blocks)
        near[u][at] = blocks
        near[u][later(near_pairs)] = flipped
        if step is not None:
            table[step][u][at] = blocks
            table[step][u][later(far_pairs)] = flipped

    def places(group):
        return pl.ds(group * pair_group, pair_group), lambda by: pl.ds(by + group * pair_group, pair_group)

    groups = row_pairs // pair_group

    def first_state(group, carry):
        at, later = places(group)
        blocks = teleports[at]
        for u in range(HALVES):
            keep_state(0, u, at, later, blocks[:, u])
        return carry

    lax.fori_loop(0, groups, first_state, 0)
    to_scalars.wait()

    def exchange(step, u, first, count):
        at = pl.ds(first * PAIRS, count * PAIRS)
        if step < STEPS:
            dst = table[step][u].at[pl.ds(row_pairs + first * PAIRS, count * PAIRS)]
        else:
            dst = back_buf.at[step - STEPS, u, at]
        return pltpu.make_async_remote_copy(
            src_ref=out_buf.at[step, u, at],
            dst_ref=dst,
            send_sem=send_sems.at[step, u],
            recv_sem=recv_sems.at[step, u],
            device_id={"dom": dom_at(first + 1)},
            device_id_type=MESH,
        )

    def two(source, a, b):
        return jnp.where(low, source[a], source[b])

    def send_state(step, u):
        def send(i, carry):
            k = mixed(i)
            asked = [want_s[peers - 1 - k, 0, HALF * c] for c in range(CAP)]
            ready = [two(near[u], asked[2 * t], asked[2 * t + 1]) for t in range(PAIRS)]
            out_buf[step, u, pl.ds(k * PAIRS, PAIRS)] = jnp.stack(ready)
            exchange(step, u, k, 1).start()
            return carry

        lax.fori_loop(0, peers, send, 0)

    for u in range(HALVES):
        send_state(0, u)

    loads[3].wait()

    def rearrange(group, carry):
        rows = BLOCK * BLOCK // LANES
        first = pl.multiple_of(group * SPREAD, SPREAD)
        for m in range(rows):
            part = values_here[pl.ds(first, SPREAD), m * LANES : (m + 1) * LANES]
            by_entry[pl.ds(m, SPREAD, stride=rows), :] = part.astype(F32)
        left = lax.broadcasted_iota(jnp.int32, (rows, LANES), 1) < BLOCK
        for pair in range(SPREAD // 2):
            one = by_entry[2 * pair * rows : (2 * pair + 1) * rows, :]
            two_ = by_entry[(2 * pair + 1) * rows : (2 * pair + 2) * rows, :]
            by_row[pl.ds(pair * BLOCK, rows, stride=2), :] = jnp.where(left, one, swap(two_))
            by_row[pl.ds(pair * BLOCK + 1, rows, stride=2), :] = jnp.where(left, swap(one), two_)
        for pair in range(SPREAD // 2):
            tiles[group * (SPREAD // 2) + pair] = by_row[pair * BLOCK : (pair + 1) * BLOCK, :].astype(BF16)
        return carry

    lax.fori_loop(0, entries // SPREAD, rearrange, 0)

    def row_tiles(r):
        return jnp.concatenate([tiles[4 * r + q] for q in range(4)], axis=1)

    contract_lanes = (((1,), (1,)), ((), ()))
    ones = jnp.ones((HALF, 4 * LANES), BF16)

    def row_products(left, r):
        return lax.dot_general(left, row_tiles(r), contract_lanes, preferred_element_type=F32)

    def degree(group, carry):
        sums = [row_products(ones, group * GROUP + i) for i in range(GROUP)]
        sums = jnp.stack([jnp.concatenate(sums[2 * i : 2 * i + 2], axis=1) for i in range(pair_group)])
        inverse[pl.ds(group * pair_group, pair_group)] = 1.0 / (1.0 + sums)
        return carry

    lax.fori_loop(0, groups, degree, 0)

    side_of = jnp.where(lax.broadcasted_iota(jnp.int32, (BLOCK, LANES), 1) < BLOCK, 0, 1)

    def build_tiles(dst, group, at_start, at_code):
        made = []
        for i in range(4):
            pair, coded = tiles[index[at_start + 4 * group + i]].astype(F32), index[at_code + 4 * group + i]
            turned = jnp.where(side_of == coded - 4, swap(pair), 0.0)
            made.append(jnp.where(side_of == coded, pair, turned).astype(BF16))
        at = pl.ds(pl.multiple_of(group * 4 * BLOCK, 4 * BLOCK), 4 * BLOCK)
        dst[at, :] = jnp.concatenate(made, axis=0)

    def build_remote(group, carry):
        build_tiles(remote_tiles, group, at_slot_tile, at_slot_side)
        return carry

    def build_local(group, carry):
        build_tiles(local_tiles, group, at_tile, at_side)
        return carry

    route_rows = 2 * row_pairs * HALF

    def build_route(m, carry):
        row = lax.broadcasted_iota(jnp.int32, (route_rows, LANES), 0)
        col = lax.broadcasted_iota(jnp.int32, (route_rows, LANES), 1)
        wide = lax.broadcasted_iota(jnp.int32, (1, LANES), 1) < BLOCK
        asked = jnp.where(wide, want[2 * m], want[2 * m + 1])
        target = jnp.where(asked < row_pairs, asked, jnp.where(asked == row_pairs, -row_pairs, asked - 1))
        hit = row - col % HALF == target * HALF
        at = pl.ds(pl.multiple_of(m * route_rows, route_rows), route_rows)
        route[at, :] = jnp.where(hit, 1.0, 0.0).astype(BF16)
        return carry

    def show(out, u, group, blocks):
        for i in range(pair_group):
            at = pl.ds(pl.multiple_of((group * pair_group + i) * LANES, LANES), LANES)
            out[u * HALF : (u + 1) * HALF, at] = blocks[i]

    for step in range(STEPS):
        for u in range(HALVES):
            if (step, u) == (1, 0):
                lax.fori_loop(0, chunks // 4, build_local, 0)
            elif (step, u) == (1, 1):
                lax.fori_loop(chunks // 4, chunks // 2, build_local, 0)
            elif (step, u) == (2, 0):
                lax.fori_loop(0, peers, build_remote, 0)
            elif (step, u) == (2, 1):
                lax.fori_loop(0, doms // 2, build_route, 0)
                acc[chunks] = jnp.zeros((HALF, LANES), F32)
                blank = jnp.zeros((PAIRS, HALF, LANES), BF16)
                for late in range(STEPS):
                    for v in range(HALVES):
                        back_buf[late, v, pl.ds(peers * PAIRS, PAIRS)] = blank
            exchange(step, u, 0, peers).wait_recv()
            here = table[step][u]

            def turn_some(first, count):
                here[pl.ds(far_pairs + first, count)] = turn(here[pl.ds(first, count)])

            def turn_group(group, carry):
                turn_some(row_pairs + group * 2 * GROUP, 2 * GROUP)
                return carry

            whole_groups = peers * PAIRS // (2 * GROUP)
            lax.fori_loop(0, whole_groups, turn_group, 0)
            done = whole_groups * 2 * GROUP
            turn_some(row_pairs + done, peers * PAIRS - done)

            def propagate(group, carry):
                sums = []
                for i in range(GROUP):
                    r = group * GROUP + i
                    picked = [two(here, index[8 * r + 2 * q], index[8 * r + 2 * q + 1]) for q in range(4)]
                    sums.append(row_products(jnp.concatenate(picked, axis=1), r))
                sums = jnp.stack([jnp.concatenate(sums[2 * i : 2 * i + 2], axis=1) for i in range(pair_group)])
                at, later = places(group)
                rounded, teleport = near[u][at].astype(F32), teleports[at, u].astype(F32)
                state = (1.0 - TELEPORT) * ((sums + rounded) * inverse[at]) + TELEPORT * teleport
                if step + 1 < STEPS:
                    keep_state(step + 1, u, at, later, state.astype(BF16))
                else:
                    final[u, at] = state
                    show(prop_out, u, group, state)
                return carry

            lax.fori_loop(0, groups, propagate, 0)
            if step + 1 < STEPS:
                send_state(step + 1, u)

    def class_id(u):
        return my_col * share + u * HALF + lax.broadcasted_iota(jnp.int32, (HALF, LANES), 0)

    state = [final[u] for u in range(HALVES)]
    usable = [class_id(u) < classes for u in range(HALVES)]
    top = functools.reduce(
        jnp.maximum, [jnp.max(jnp.where(usable[u], state[u], FILL), axis=1) for u in range(HALVES)]
    )
    sums = functools.reduce(
        jnp.add,
        [
            jnp.sum(jnp.where(usable[u], jnp.exp(state[u] - top[:, None, :]), 0.0), axis=1)
            for u in range(HALVES)
        ],
    )
    stat_send[0] = top
    stat_send[1] = sums

    def stat_copy(j):
        return pltpu.make_async_remote_copy(
            src_ref=stat_send,
            dst_ref=stat_recv.at[j],
            send_sem=stat_sems.at[0, j],
            recv_sem=stat_sems.at[1, j],
            device_id={"col": col_at(j + 1)},
            device_id_type=MESH,
        )

    for j in range(cols - 1):
        stat_copy(j).start()
    for j in range(cols - 1):
        stat_copy(j).wait_recv()
    tops = [stat_send[0]] + [stat_recv[j, 0] for j in range(cols - 1)]
    sums = [stat_send[1]] + [stat_recv[j, 1] for j in range(cols - 1)]
    top = functools.reduce(jnp.maximum, tops)
    whole = functools.reduce(jnp.add, [s * jnp.exp(t - top) for s, t in zip(sums, tops)])
    stat_recv[0, 0] = top
    stat_recv[0, 1] = 1.0 / whole

    def send_products(late, u):
        def products_for(k):
            ready = []
            for t in range(PAIRS):
                slot = at_slot_row + CAP * k + 2 * t
                at = pl.ds(pl.multiple_of((k * PAIRS + t) * LANES, LANES), LANES)
                left = two(near[u], index[slot], index[slot + 1])
                ready.append(jnp.dot(left, remote_tiles[at, :], preferred_element_type=F32))
            return jnp.stack(ready).astype(BF16)

        def send(first, count):
            order = [mixed(first + i) for i in range(count)]
            ready = [products_for(k) for k in order]
            for k, blocks in zip(order, ready):
                out_buf[STEPS + late, u, pl.ds(k * PAIRS, PAIRS)] = blocks
            for k in order:
                exchange(STEPS + late, u, k, 1).start()

        def send_group(group, carry):
            send(group * 4, 4)
            return carry

        lax.fori_loop(0, peers // 4, send_group, 0)
        send(peers // 4 * 4, peers % 4)

    for u in range(HALVES):

        def cotangent(group, carry):
            at, later = places(group)
            rows = pl.ds(group * pair_group, pair_group)
            expo = jnp.exp(final[u, at] - stat_recv[0, 0, rows, :][:, None, :])
            probs = expo * stat_recv[0, 1, rows, :][:, None, :]
            coded = code[at]
            onehot = jnp.where(class_id(u) == coded % 256, 1.0, 0.0)
            weight = (coded // 256).astype(F32)
            gradient = jnp.where(usable[u], weight * (probs - onehot), 0.0)
            grad[u, at] = TELEPORT * gradient
            keep_state(None, u, at, later, (inverse[at] * gradient).astype(BF16))
            return carry

        lax.fori_loop(0, groups, cotangent, 0, unroll=True)
        send_products(0, u)

    for late in range(STEPS):
        for u in range(HALVES):

            def local_chunks(group, running):
                terms = []
                for i in range(GROUP):
                    m = group * GROUP + i
                    left = two(near[u], index[at_row + 2 * m], index[at_row + 2 * m + 1])
                    weights = local_tiles[pl.ds(pl.multiple_of(m * LANES, LANES), LANES), :]
                    terms.append(jnp.dot(left, weights, preferred_element_type=F32))
                sums = []
                for i in range(GROUP):
                    running = running * index[at_keep + group * GROUP + i].astype(F32) + terms[i]
                    sums.append(running)
                acc[pl.ds(group * GROUP, GROUP)] = jnp.stack(sums)
                return running

            lax.fori_loop(0, chunks // GROUP, local_chunks, jnp.zeros((HALF, LANES), F32))

            def local_sum(group, carry):
                picked = [acc[index[at_last + group * GROUP + i]] for i in range(GROUP)]
                come_in[pl.ds(group * pair_group, pair_group)] = jnp.stack(
                    [picked[2 * i] + picked[2 * i + 1] for i in range(pair_group)]
                )
                return carry

            lax.fori_loop(0, groups, local_sum, 0)
            exchange(STEPS + late, u, 0, peers).wait_recv()

            def arrive(m, carry):
                first = [pl.multiple_of((2 * m + i) * route_rows, route_rows) for i in range(2)]
                left = jnp.concatenate([route[pl.ds(f, route_rows), :] for f in first], axis=1)
                part = back_buf[late, u, pl.ds(m * 4 * PAIRS, 4 * PAIRS)]
                none = jnp.zeros_like(part)
                part = jnp.stack([jnp.where(low, part, none), jnp.where(low, none, part)], axis=1)
                sums = jnp.dot(left, part.reshape(4 * CAP * HALF, LANES), preferred_element_type=F32)
                own_half, other = sums[: route_rows // 2], swap(sums[route_rows // 2 :])
                come_in[...] += (own_half + other).reshape(row_pairs, HALF, LANES)
                return carry

            lax.fori_loop(0, doms // 4, arrive, 0)

            def finish(group, carry):
                at, later = places(group)
                gradient = (1.0 - TELEPORT) * (come_in[at] + near[u][at].astype(F32))
                if late < STEPS - 1:
                    grad[u, at] += TELEPORT * gradient
                    keep_state(None, u, at, later, (inverse[at] * gradient).astype(BF16))
                else:
                    show(grad_out, u, group, grad[u, at] + gradient)
                return carry

            lax.fori_loop(0, groups, finish, 0)
            if late < STEPS - 1:
                send_products(late + 1, u)

    all_requests().wait_send()
    for j in range(cols - 1):
        head_copy(j).wait_send()
        stat_copy(j).wait_send()
    for step in range(2 * STEPS):
        for u in range(HALVES):
            exchange(step, u, 0, peers).wait_send()


def body(features, w_hidden, w_out, block_values, block_slot, requested, labels, train_mask):
    doms, cols = lax.axis_size("dom"), lax.axis_size("col")
    nodes = labels.shape[0]
    row_blocks = nodes // BLOCK
    row_pairs = row_blocks // 2
    share = w_out.shape[1] // cols
    entries = block_slot.shape[0]
    index, chunks = index_tables(block_slot, doms, row_blocks)
    side = jnp.arange(CAP, dtype=jnp.int32) % 2
    asked = requested // 2 + jnp.where(requested % 2 == side, 0, row_pairs + 1)
    asked = jnp.where(requested < 0, row_pairs, asked)
    request = jnp.broadcast_to(asked.reshape(doms, 1, 1, CAP, 1), (doms, 1, 2, CAP, HALF)).reshape(doms, 1, LANES)
    code = (labels + 256 * train_mask).reshape(row_pairs, 1, LANES)
    peers = doms - 1
    far_pairs = row_pairs + peers * PAIRS
    rows = BLOCK * BLOCK // LANES
    mine = features.shape[0] // LANES
    vmem, dma = pltpu.VMEM, pltpu.SemaphoreType.DMA
    block = (HALF, LANES)
    in_vmem = pl.BlockSpec(memory_space=pltpu.VMEM)
    anywhere = pl.BlockSpec(memory_space=pl.ANY)
    return pl.pallas_call(
        functools.partial(kernel, doms, cols, NCLASS, chunks),
        out_shape=[jax.ShapeDtypeStruct((share, nodes), F32)] * 2,
        in_specs=[pl.BlockSpec(memory_space=pltpu.SMEM)] + [anywhere] * 4 + [in_vmem] * 2,
        out_specs=[in_vmem] * 2,
        scratch_shapes=[
            vmem(features.shape, BF16),
            vmem(w_hidden.shape, BF16),
            vmem(w_out.shape, BF16),
            vmem((entries, BLOCK * BLOCK), BF16),
            vmem((SPREAD * rows, LANES), F32),
            vmem((SPREAD * rows, LANES), F32),
            vmem((entries // 2, BLOCK, LANES), BF16),
            vmem((cols * mine, HALVES, *block), BF16),
            vmem((2, row_pairs, LANES), F32),
            vmem((cols - 1, 2, row_pairs, LANES), F32),
            vmem((doms, 1, LANES), jnp.int32),
            pltpu.SMEM((doms, 1, LANES), jnp.int32),
            vmem((row_pairs, HALVES, *block), BF16),
            *[vmem((2 * far_pairs, *block), BF16) for _ in range(STEPS * HALVES)],
            *[vmem((2 * (row_pairs + 1), *block), BF16) for _ in range(HALVES)],
            vmem((row_pairs, *block), F32),
            vmem((HALVES, row_pairs, *block), F32),
            vmem((HALVES, row_pairs, *block), F32),
            vmem((chunks + 1, *block), F32),
            vmem((row_pairs, *block), F32),
            vmem((peers * CAP * BLOCK, LANES), BF16),
            vmem((2 * chunks * BLOCK, LANES), BF16),
            vmem((doms // 2 * 2 * row_pairs * HALF, LANES), BF16),
            vmem((2 * STEPS, HALVES, peers * PAIRS, *block), BF16),
            vmem((STEPS, HALVES, doms * PAIRS, *block), BF16),
            dma((2, cols - 1)),
            dma((2, cols - 1)),
            dma((2,)),
            dma((5,)),
            dma((2 * STEPS, HALVES)),
            dma((2 * STEPS, HALVES)),
        ],
        compiler_params=pltpu.CompilerParams(
            collective_id=0, has_side_effects=True, vmem_limit_bytes=48 * 2**20
        ),
    )(index, features, w_hidden, w_out, block_values, request, code)


def solution(mesh):
    return jax.shard_map(
        body,
        mesh=mesh,
        in_specs=(
            P(("dom", "col"), None),
            P(),
            P(),
            P("dom", None),
            P("dom"),
            P("dom", None, None),
            P("dom"),
            P("dom"),
        ),
        out_specs=(P("col", "dom"), P("col", "dom")),
        check_vma=False,
    )
```

profile of v0, /device:TPU:1, one launch (start us, length us, event | category | flops | bytes accessed | tf_op | source)
XLA Modules:
  0.0 122.5 jit_solution(14059795091489783336)
XLA Ops:
  0.6 0.8 convert_reduce_fusion.1
  1.4 0.1 select_reduce_fusion.3
  1.6 0.8 select_reduce_fusion.2
  2.3 0.1 convert_reduce_fusion.2
  2.4 0.9 convert_reduce_fusion
  3.4 0.8 fusion.4
  4.1 0.7 multiply_add_fusion
  4.9 0.7 add_select_fusion.2
  5.6 0.1 select_reduce_fusion
  5.7 0.1 select_reduce_fusion.1
  6.0 0.1 copy.12.request
  6.0 0.0 copy-start
  6.0 1.6 %copy-done = bf16[256,4096]{1,0:T(8,128)(2,1)S(1)} copy-done((bf16[256,4096]{1,0:T(8,128)(2,1)S(1)}, bf16[256,4096]{1,0:T(8,128)(2,1)}, u32[]{:S(2)}) %copy-start) | copy-done | bytes 2097176
  7.7 0.0 copy-start.1
  7.7 0.9 copy-done.1
  8.6 0.0 copy-start.2
  8.6 0.8 copy-done.2
  9.4 0.0 copy-start.3
  9.4 0.8 copy-done.3
  10.2 110.8 %shard_map.95 = (f32[32,2048]{1,0:T(8,128)S(1)}, f32[32,2048]{1,0:T(8,128)S(1)}) custom-call(s32[1568]{0:T(1024)S(1)} %constant_dynamic-update-slice_fusion.index, bf16[256,128]{1,0:T(8,128)(2,1)S(1)} %copy-done.2, bf16[128,256]{1,0:T(8,128)(2,1)S(1)} %copy-done.3, bf16[256,256]{1,0:T(8,128)(2,1)S(1)} %copy-done.1, bf16[256,4096]{1,0:T(8,128)(2,1)S(1)} %copy-done, ...), custom_call_target="tpu_custom_call" | custom-call | tf_op jit(solution)/shard_map/pallas_call | solution.py:606
  121.1 0.7 copy.24
  121.8 0.7 copy.25
  (13 shorter events, 0.2 us)
Async XLA Ops:
  6.0 1.6 %copy-start = (bf16[256,4096]{1,0:T(8,128)(2,1)S(1)}, bf16[256,4096]{1,0:T(8,128)(2,1)}, u32[]{:S(2)}) copy-start(bf16[256,4096]{1,0:T(8,128)(2,1)} %values.1) | copy-start | bytes 6291460
  7.7 0.9 copy-start.1
  8.6 0.8 copy-start.2
  9.4 0.8 copy-start.3
where the time goes:
time: 123 us; the launch traced here: 122 us
  Pallas kernels  111 us (90%)
  local copies, waits for them, and re-layouts  5.66 us (5%)
  other arithmetic  5.28 us (4%)
    pallas_call x1, Pallas kernels, body(): pl.pallas_call(functools.partial(kernel, doms, cols, NCLASS, chunks), out...  111 us
    unnamed x10, local copies, waits for them, and re-layouts  5.6 us

commit v1 on v0

--- a/solution.py
+++ b/solution.py
@@ -366,14 +366,14 @@
         build_tiles(local_tiles, group, at_tile, at_side)
         return carry
 
-    route_rows = 2 * row_pairs * HALF
+    route_rows = row_pairs * HALF
 
     def build_route(m, carry):
         row = lax.broadcasted_iota(jnp.int32, (route_rows, LANES), 0)
         col = lax.broadcasted_iota(jnp.int32, (route_rows, LANES), 1)
         wide = lax.broadcasted_iota(jnp.int32, (1, LANES), 1) < BLOCK
         asked = jnp.where(wide, want[2 * m], want[2 * m + 1])
-        target = jnp.where(asked < row_pairs, asked, jnp.where(asked == row_pairs, -row_pairs, asked - 1))
+        target = jnp.where(asked < row_pairs, asked, jnp.where(asked == row_pairs, -row_pairs, asked - near_pairs))
         hit = row - col % HALF == target * HALF
         at = pl.ds(pl.multiple_of(m * route_rows, route_rows), route_rows)
         route[at, :] = jnp.where(hit, 1.0, 0.0).astype(BF16)
@@ -517,6 +517,9 @@
         lax.fori_loop(0, groups, cotangent, 0, unroll=True)
         send_products(0, u)
 
+    nothing = jnp.zeros((HALF, LANES), BF16)
+    half_of = jnp.where(low, 0, 1)
+
     for late in range(STEPS):
         for u in range(HALVES):
 
@@ -550,11 +553,15 @@
                 first = [pl.multiple_of((2 * m + i) * route_rows, route_rows) for i in range(2)]
                 left = jnp.concatenate([route[pl.ds(f, route_rows), :] for f in first], axis=1)
                 part = back_buf[late, u, pl.ds(m * 4 * PAIRS, 4 * PAIRS)]
-                none = jnp.zeros_like(part)
-                part = jnp.stack([jnp.where(low, part, none), jnp.where(low, none, part)], axis=1)
-                sums = jnp.dot(left, part.reshape(4 * CAP * HALF, LANES), preferred_element_type=F32)
-                own_half, other = sums[: route_rows // 2], swap(sums[route_rows // 2 :])
-                come_in[...] += (own_half + other).reshape(row_pairs, HALF, LANES)
+                flipped = turn(part)
+                both = jnp.where(low, part, flipped), jnp.where(low, flipped, part)
+                rows = []
+                for i in range(4 * CAP):
+                    asked = want_s[4 * m + i // CAP, 0, HALF * (i % CAP)]
+                    goal = jnp.where(asked < near_pairs, i % 2, 1 - i % 2)
+                    rows.append(jnp.where(half_of == goal, both[i % 2][i // 2], nothing))
+                sums = jnp.dot(left, jnp.concatenate(rows, axis=0), preferred_element_type=F32)
+                come_in[...] += sums.reshape(row_pairs, HALF, LANES)
                 return carry
 
             lax.fori_loop(0, doms // 4, arrive, 0)
@@ -631,7 +638,7 @@
             vmem((row_pairs, *block), F32),
             vmem((peers * CAP * BLOCK, LANES), BF16),
             vmem((2 * chunks * BLOCK, LANES), BF16),
-            vmem((doms // 2 * 2 * row_pairs * HALF, LANES), BF16),
+            vmem((doms // 2 * row_pairs * HALF, LANES), BF16),
             vmem((2 * STEPS, HALVES, peers * PAIRS, *block), BF16),
             vmem((STEPS, HALVES, doms * PAIRS, *block), BF16),
             dma((2, cols - 1)),

time: 123 us -> 120 us (0.976)
  Pallas kernels: 111 us -> 108 us
    pallas_call x1, Pallas kernels: 111 us -> 108 us  [body(): pl.pallas_call(functools.partial(kernel, doms, cols, NCLASS, chunks), out...]
where the time goes in v1:
time: 120 us
  Pallas kernels  108 us (90%)
  local copies, waits for them, and re-layouts  5.66 us (5%)
  other arithmetic  5.28 us (4%)
    pallas_call x1, Pallas kernels, body(): pl.pallas_call(functools.partial(kernel, doms, cols, NCLASS, chunks), out...  108 us
    unnamed x10, local copies, waits for them, and re-layouts  5.6 us

profile of v1, /device:TPU:1, one launch (start us, length us, event | category | flops | bytes accessed | tf_op | source)
XLA Modules:
  0.0 119.8 jit_solution(16313334226326260802)
XLA Ops:
  0.6 0.8 convert_reduce_fusion.1
  1.4 0.1 select_reduce_fusion.3
  1.6 0.8 select_reduce_fusion.2
  2.3 0.1 convert_reduce_fusion.2
  2.4 0.9 convert_reduce_fusion
  3.4 0.8 fusion.4
  4.1 0.7 multiply_add_fusion
  4.9 0.7 add_select_fusion.2
  5.6 0.1 select_reduce_fusion
  5.7 0.1 select_reduce_fusion.1
  6.0 0.1 copy.12.request
  6.0 0.0 copy-start
  6.0 1.6 %copy-done = bf16[256,4096]{1,0:T(8,128)(2,1)S(1)} copy-done((bf16[256,4096]{1,0:T(8,128)(2,1)S(1)}, bf16[256,4096]{1,0:T(8,128)(2,1)}, u32[]{:S(2)}) %copy-start) | copy-done | bytes 2097176
  7.7 0.0 copy-start.1
  7.7 0.9 copy-done.1
  8.6 0.0 copy-start.2
  8.6 0.8 copy-done.2
  9.4 0.0 copy-start.3
  9.4 0.8 copy-done.3
  10.2 108.1 %shard_map.95 = (f32[32,2048]{1,0:T(8,128)S(1)}, f32[32,2048]{1,0:T(8,128)S(1)}) custom-call(s32[1568]{0:T(1024)S(1)} %constant_dynamic-update-slice_fusion.index, bf16[256,128]{1,0:T(8,128)(2,1)S(1)} %copy-done.2, bf16[128,256]{1,0:T(8,128)(2,1)S(1)} %copy-done.3, bf16[256,256]{1,0:T(8,128)(2,1)S(1)} %copy-done.1, bf16[256,4096]{1,0:T(8,128)(2,1)S(1)} %copy-done, ...), custom_call_target="tpu_custom_call" | custom-call | tf_op jit(solution)/shard_map/pallas_call | solution.py:613
  118.4 0.7 copy.24
  119.1 0.7 copy.25
  (13 shorter events, 0.2 us)
Async XLA Ops:
  6.0 1.6 %copy-start = (bf16[256,4096]{1,0:T(8,128)(2,1)S(1)}, bf16[256,4096]{1,0:T(8,128)(2,1)}, u32[]{:S(2)}) copy-start(bf16[256,4096]{1,0:T(8,128)(2,1)} %values.1) | copy-start | bytes 6291460
  7.7 0.9 copy-start.1
  8.6 0.8 copy-start.2
  9.4 0.8 copy-start.3

commit v2 on v1

--- a/solution.py
+++ b/solution.py
@@ -296,16 +296,30 @@
     def two(source, a, b):
         return jnp.where(low, source[a], source[b])
 
+    def in_groups(send):
+        def send_group(group, carry):
+            send(group * GROUP, GROUP)
+            return carry
+
+        lax.fori_loop(0, peers // GROUP, send_group, 0)
+        send(peers // GROUP * GROUP, peers % GROUP)
+
+    def send_all(step, u, blocks_for):
+        def send(first, count):
+            order = [mixed(first + i) for i in range(count)]
+            ready = [blocks_for(k) for k in order]
+            for k, blocks in zip(order, ready):
+                out_buf[step, u, pl.ds(k * PAIRS, PAIRS)] = blocks
+                exchange(step, u, k, 1).start()
+
+        in_groups(send)
+
     def send_state(step, u):
-        def send(i, carry):
-            k = mixed(i)
+        def blocks_for(k):
             asked = [want_s[peers - 1 - k, 0, HALF * c] for c in range(CAP)]
-            ready = [two(near[u], asked[2 * t], asked[2 * t + 1]) for t in range(PAIRS)]
-            out_buf[step, u, pl.ds(k * PAIRS, PAIRS)] = jnp.stack(ready)
-            exchange(step, u, k, 1).start()
-            return carry
-
-        lax.fori_loop(0, peers, send, 0)
+            return jnp.stack([two(near[u], asked[2 * t], asked[2 * t + 1]) for t in range(PAIRS)])
+
+        send_all(step, u, blocks_for)
 
     for u in range(HALVES):
         send_state(0, u)
@@ -484,20 +498,7 @@
                 ready.append(jnp.dot(left, remote_tiles[at, :], preferred_element_type=F32))
             return jnp.stack(ready).astype(BF16)
 
-        def send(first, count):
-            order = [mixed(first + i) for i in range(count)]
-            ready = [products_for(k) for k in order]
-            for k, blocks in zip(order, ready):
-                out_buf[STEPS + late, u, pl.ds(k * PAIRS, PAIRS)] = blocks
-            for k in order:
-                exchange(STEPS + late, u, k, 1).start()
-
-        def send_group(group, carry):
-            send(group * 4, 4)
-            return carry
-
-        lax.fori_loop(0, peers // 4, send_group, 0)
-        send(peers // 4 * 4, peers % 4)
+        send_all(STEPS + late, u, products_for)
 
     for u in range(HALVES):
 

time: 120 us -> 118 us (0.983)
  Pallas kernels: 108 us -> 106 us
    pallas_call x1, Pallas kernels: 108 us -> 106 us  [body(): pl.pallas_call(functools.partial(kernel, doms, cols, NCLASS, chunks), out...]
where the time goes in v2:
time: 118 us
  Pallas kernels  106 us (90%)
  local copies, waits for them, and re-layouts  5.66 us (5%)
  other arithmetic  5.28 us (4%)
    pallas_call x1, Pallas kernels, body(): pl.pallas_call(functools.partial(kernel, doms, cols, NCLASS, chunks), out...  106 us
    unnamed x10, local copies, waits for them, and re-layouts  5.6 us

profile of v2, /device:TPU:1, one launch (start us, length us, event | category | flops | bytes accessed | tf_op | source)
XLA Modules:
  0.0 117.6 jit_solution(7166132755524594314)
XLA Ops:
  0.6 0.8 convert_reduce_fusion.1
  1.4 0.1 select_reduce_fusion.3
  1.6 0.8 select_reduce_fusion.2
  2.3 0.1 convert_reduce_fusion.2
  2.4 0.9 convert_reduce_fusion
  3.4 0.8 fusion.4
  4.1 0.7 multiply_add_fusion
  4.9 0.7 add_select_fusion.2
  5.6 0.1 select_reduce_fusion
  5.7 0.1 select_reduce_fusion.1
  6.0 0.1 copy.12.request
  6.0 0.0 copy-start
  6.0 1.6 %copy-done = bf16[256,4096]{1,0:T(8,128)(2,1)S(1)} copy-done((bf16[256,4096]{1,0:T(8,128)(2,1)S(1)}, bf16[256,4096]{1,0:T(8,128)(2,1)}, u32[]{:S(2)}) %copy-start) | copy-done | bytes 2097176
  7.7 0.0 copy-start.1
  7.7 0.9 copy-done.1
  8.6 0.0 copy-start.2
  8.6 0.8 copy-done.2
  9.4 0.0 copy-start.3
  9.4 0.8 copy-done.3
  10.2 106.0 %shard_map.95 = (f32[32,2048]{1,0:T(8,128)S(1)}, f32[32,2048]{1,0:T(8,128)S(1)}) custom-call(s32[1568]{0:T(1024)S(1)} %constant_dynamic-update-slice_fusion.index, bf16[256,128]{1,0:T(8,128)(2,1)S(1)} %copy-done.2, bf16[128,256]{1,0:T(8,128)(2,1)S(1)} %copy-done.3, bf16[256,256]{1,0:T(8,128)(2,1)S(1)} %copy-done.1, bf16[256,4096]{1,0:T(8,128)(2,1)S(1)} %copy-done, ...), custom_call_target="tpu_custom_call" | custom-call | tf_op jit(solution)/shard_map/pallas_call | solution.py:614
  116.2 0.7 copy.24
  116.9 0.7 copy.25
  (13 shorter events, 0.2 us)
Async XLA Ops:
  6.0 1.6 %copy-start = (bf16[256,4096]{1,0:T(8,128)(2,1)S(1)}, bf16[256,4096]{1,0:T(8,128)(2,1)}, u32[]{:S(2)}) copy-start(bf16[256,4096]{1,0:T(8,128)(2,1)} %values.1) | copy-start | bytes 6291460
  7.7 0.9 copy-start.1
  8.6 0.8 copy-start.2
  9.4 0.8 copy-start.3
